TPU v7x, 32 devices: a whole 2x2x4 slice. The times are simulated.
32 devices in a mesh: dp: 8 (over z, x), expert: 4 (over y, core).
Axes of the slice: x: 2, y: 2, z: 4, core: 2. Of those that a mesh axis runs over, the one named last changes fastest.
Arguments:
- grad_out: bfloat16 [4096, 1536], P(('dp', 'expert')), may hold values from -6 to 6
- expert_ids: int32 [4096, 2], P(('dp', 'expert')), may hold values from 0 to 3, all different within a row; in each aligned block of 128 rows (0 to 127, 128 to 255, ...) at most 96 rows name the same one
- gates: float32 [4096, 2], P(('dp', 'expert')), may hold values from 0.1 to 1
- routed_pre: bfloat16 [8, 4, 384, 3072], P('dp', 'expert'), may hold values from -6 to 6
- routed_down: bfloat16 [4, 3072, 1536], P('expert', 'dp'), may hold values from -0.109375 to 0.109375
- shared_pre: bfloat16 [4096, 6144], P('dp', 'expert'), may hold values from -6 to 6
- shared_down: bfloat16 [6144, 1536], P(('expert', 'dp')), may hold values from -0.078125 to 0.078125
Outputs:
- routed_pre_grad: bfloat16 [8, 4, 384, 3072], P('dp', 'expert')
- routed_down_grad: float32 [4, 3072, 1536], P('expert', 'dp')
- shared_pre_grad: bfloat16 [4096, 6144], P('dp', 'expert')
- shared_down_grad: float32 [6144, 1536], P(('expert', 'dp'))
- gate_grad: float32 [4096, 2], P(('dp', 'expert'))
Inputs may be any that keep to these rules, and one draw needn't show every extreme that they name: `expert_ids`: each row names two different experts. Among the 128 rows of one device no expert is named more than 96 times, and in every draw some expert is named exactly 96 times by the rows of some device.
All inputs are finite; a program needn't handle non-finite values.
Results may differ from a plain program's by a relative error of at most 0.015.
Values may be sent and summed in bfloat16 or wider, within the bound.
A program may use at most 128 MiB of HBM per device.

v0:
```python
import jax
import jax.numpy as jnp
from jax import lax
from jax.sharding import PartitionSpec as P

SQRT_TWO_PI = 0.7978845608028654


def gelu_pair(inputs):
    cubic = inputs * inputs * inputs
    tangent = jnp.tanh(SQRT_TWO_PI * (inputs + 0.044715 * cubic))
    value = 0.5 * inputs * (1.0 + tangent)
    slope = 0.5 * (1.0 + tangent) + 0.5 * inputs * (1.0 - tangent * tangent) * SQRT_TWO_PI * (
        1.0 + 3.0 * 0.044715 * inputs * inputs
    )
    return (value, slope)


def slot_ranks(flat_ids, experts):
    labels = jnp.arange(experts, dtype=jnp.int32)
    onehot = (flat_ids[:, :, None] == labels[None, None, :]).astype(jnp.int32)
    before = jnp.cumsum(onehot, axis=1) - onehot
    return jnp.sum(before * onehot, axis=2)


def body(grad_out, expert_ids, gates, routed_pre, routed_down, shared_pre, shared_down):
    n_exp = lax.axis_size("expert")
    tok = grad_out.shape[0]
    width = grad_out.shape[1]
    slots = routed_pre.shape[2]
    cap = slots // n_exp
    owner = lax.axis_index("expert")
    gate_b = gates.astype(jnp.bfloat16)
    whole_down, whole_shared = (
        lax.all_gather(routed_down, "dp", axis=1, tiled=True),
        lax.all_gather(shared_down, "dp", axis=0, tiled=True),
    )
    own_rank = slot_ranks(expert_ids.reshape(1, tok * 2), n_exp).reshape(tok, 2)
    group_rows, group_gate = (
        lax.all_gather(grad_out, "expert", axis=0, tiled=True),
        lax.all_gather(gate_b, "expert", axis=0, tiled=True),
    )
    group_ids = lax.all_gather(expert_ids, "expert", axis=0, tiled=True)
    group_rank = slot_ranks(group_ids.reshape(n_exp, tok * 2), n_exp).reshape(n_exp * tok, 2)
    source = jnp.arange(n_exp * tok, dtype=jnp.int32) // tok
    target = jnp.where(group_ids == owner, source[:, None] * cap + group_rank, slots)
    recv_rows = jnp.zeros((slots + 1, width), jnp.bfloat16)
    recv_rows = recv_rows.at[target[:, 0]].set(group_rows).at[target[:, 1]].set(group_rows)[:slots]
    recv_gate = jnp.zeros((slots + 1,), jnp.bfloat16).at[target].set(group_gate)[:slots]
    value, slope = gelu_pair(routed_pre[0, 0].astype(jnp.float32))
    hidden_b = value.astype(jnp.bfloat16)
    raw = lax.dot_general(
        recv_rows, whole_down[0], (((1,), (1,)), ((), ())), preferred_element_type=jnp.float32
    )
    gate_col = recv_gate.astype(jnp.float32)[:, None]
    routed_pre_grad = (gate_col * raw * slope).astype(jnp.bfloat16).reshape(routed_pre.shape)
    slot_score = jnp.sum(value * raw, axis=1)
    scaled = (gate_col * recv_rows.astype(jnp.float32)).astype(jnp.bfloat16)
    routed_term = lax.dot_general(
        hidden_b, scaled, (((0,), (0,)), ((), ())), preferred_element_type=jnp.float32
    )
    returned = lax.all_to_all(
        slot_score.reshape(n_exp, cap), "expert", split_axis=0, concat_axis=0, tiled=True
    )
    gate_grad = returned[expert_ids, own_rank]
    svalue, sslope = gelu_pair(shared_pre.astype(jnp.float32))
    shared_b = svalue.astype(jnp.bfloat16)
    raw_shared = lax.dot_general(
        group_rows, whole_shared, (((1,), (1,)), ((), ())), preferred_element_type=jnp.float32
    )
    shared_pre_grad = (raw_shared * sslope).astype(jnp.bfloat16)
    shared_term = lax.dot_general(
        shared_b, group_rows, (((0,), (0,)), ((), ())), preferred_element_type=jnp.float32
    )
    routed_sum, shared_sum = (
        lax.psum_scatter(
            routed_term.astype(jnp.bfloat16), "dp", scatter_dimension=0, tiled=True
        ).astype(jnp.float32),
        lax.psum_scatter(
            shared_term.astype(jnp.bfloat16), "dp", scatter_dimension=0, tiled=True
        ).astype(jnp.float32),
    )
    return (
        routed_pre_grad,
        routed_sum.reshape(1, routed_sum.shape[0], width),
        shared_pre_grad,
        shared_sum,
        gate_grad,
    )


def solution(mesh):
    in_specs = (
        P(("dp", "expert"), None),
        P(("dp", "expert"), None),
        P(("dp", "expert"), None),
        P("dp", "expert", None, None),
        P("expert", "dp", None),
        P("dp", "expert"),
        P(("expert", "dp"), None),
    )
    out_specs = (
        P("dp", "expert", None, None),
        P("expert", "dp", None),
        P("dp", "expert"),
        P(("expert", "dp"), None),
        P(("dp", "expert"), None),
    )
    return jax.shard_map(body, mesh=mesh, in_specs=in_specs, out_specs=out_specs, check_vma=False)
```

profile of v0, /device:TPU:0, one launch (start us, length us, event | category | flops | bytes accessed | tf_op | source)
XLA Modules:
  0.0 525.6 jit_solution(1496746732667085062)
XLA Ops:
  7.2 0.7 all-gather.4.cloned.1.call-update
  7.9 0.7 all-gather.6.cloned.1.call-update
  8.7 0.7 all-gather.8.cloned.1.call-update
  9.4 22.5 %all-gather.4.cloned.1.call-done = bf16[512,1536]{1,0:T(8,128)(2,1)} async-done(((bf16[128,1536]{1,0:T(8,128)(2,1)}), bf16[512,1536]{1,0:T(8,128)(2,1)}) %all-gather.4.cloned.1.call-update) | async-done | bytes 1572880 | tf_op jit(solution)/shard_map/all_gather | solution.py:40
  32.0 7.3 %convolution_convert_fusion.1 = bf16[1536,1536]{1,0:T(8,128)(2,1)} fusion(bf16[512,1536]{1,0:T(8,128)(2,1)} %all-gather.4.cloned.1.call-done, bf16[512,1536]{1,0:T(8,128)(2,1)} %param.12), kind=kOutput, calls=%fused_computation.13 | convolution fusion | flops 2426142720 | bytes 7864320 | tf_op jit(solution)/shard_map/dot_general | solution.py:72
  39.3 0.6 copy-done.1
  40.1 5.8 %all_gather.15 = s32[512,2]{1,0:T(8,128)S(1)} all-gather(s32[128,2]{1,0:T(8,128)S(1)} %copy.55), channel_id=1, replica_groups=mesh['dp'=8,'expert'=4] {'expert'}, dimensions={0}, use_global_device_ids=true | all-gather | bytes 5120 | tf_op jit(solution)/shard_map/all_gather | solution.py:43
  45.8 0.2 eq.64
  46.0 0.2 eq.60
  46.2 4.8 reduce-window.14
  51.5 0.2 reshape.196
  52.1 5.0 all_gather.16
  57.1 0.2 copy.58
  57.3 0.2 reshape.219
  57.5 7.6 %scatter_custom_fusion = bf16[385]{0:T(512)(128)(2,1)S(1)} fusion(s32[1024]{0:T(1024)S(1)} %reshape.217, bf16[1024]{0:T(1024)(128)(2,1)S(1)} %reshape.219, bf16[]{:T(256)} %constant.17.clone.1), kind=kCustom, calls=%fused_computation.99 | custom fusion | bytes 772 | tf_op jit(solution)/shard_map/scatter | solution.py:49
  65.1 0.3 fusion.43
  65.4 3.4 scatter_custom_fusion.1
  68.9 3.5 scatter_fusion
  72.4 10.3 %convolution_convert_fusion = bf16[3072,1536]{1,0:T(8,128)(2,1)} fusion(bf16[1,1,384,3072]{3,2,1,0:T(8,128)(2,1)} %param.10, f32[384]{0:T(512)S(1)} %slice_convert_fusion, bf16[385,1536]{1,0:T(8,128)(2,1)S(1)} %scatter_fusion), kind=kOutput, calls=%fused_computation.4 | convolution fusion | flops 3642163200 | bytes 12978176 | tf_op jit(solution)/shard_map/dot_general | solution.py:59
  82.9 1.2 reduce-window.16
  85.0 87.2 %all-gather.6.cloned.1.call-done = bf16[1,3072,1536]{2,1,0:T(8,128)(2,1)} async-done(((bf16[1,384,1536]{2,1,0:T(8,128)(2,1)}), bf16[1,3072,1536]{2,1,0:T(8,128)(2,1)}) %all-gather.6.cloned.1.call-update) | async-done | bytes 9437200 | tf_op jit(solution)/shard_map/all_gather | solution.py:35
  172.2 10.1 %multiply_reduce_fusion = (f32[384]{0:T(512)S(1)}, bf16[1,1,384,3072]{3,2,1,0:T(8,128)(2,1)}) fusion(bf16[1,1,384,3072]{3,2,1,0:T(8,128)(2,1)} %param.10, f32[384]{0:T(512)S(1)} %slice_convert_fusion, bf16[1,3072,1536]{2,1,0:T(8,128)(2,1)} %all-gather.6.cloned.1.call-done, bf16[385,1536]{1,0:T(8,128)(2,1)S(1)} %scatter_fusion), kind=kOutput, calls=%fused_computation.31 | convolution fusion | flops 3652189696 | bytes 15339008 | tf_op jit(solution)/shard_map/dot_general | solution.py:52
  182.3 0.7 all_to_all.8
  183.0 3.4 all-to-all-start
  186.5 66.1 %all-gather.8.cloned.1.call-done = bf16[1536,1536]{1,0:T(8,128)(2,1)} async-done(((bf16[192,1536]{1,0:T(8,128)(2,1)}), bf16[1536,1536]{1,0:T(8,128)(2,1)}) %all-gather.8.cloned.1.call-update) | async-done | bytes 4718608 | tf_op jit(solution)/shard_map/all_gather | solution.py:36
  252.5 7.4 %fusion.24 = bf16[512,1536]{1,0:T(8,128)(2,1)} fusion(bf16[512,1536]{1,0:T(8,128)(2,1)} %param.12, bf16[512,1536]{1,0:T(8,128)(2,1)S(1)} %copy-done, bf16[1536,1536]{1,0:T(8,128)(2,1)} %all-gather.8.cloned.1.call-done), kind=kOutput, calls=%fused_computation.44 | convolution fusion | flops 2431647744 | bytes 9437184 | tf_op jit(solution)/shard_map/dot_general | solution.py:68
  260.0 89.5 %reduce-scatter.5.cloned.1.call-done = bf16[192,1536]{1,0:T(8,128)(2,1)} async-done(((bf16[1536,1536]{1,0:T(8,128)(2,1)}), bf16[192,1536]{1,0:T(8,128)(2,1)}) %reduce-scatter.5.cloned.1.call-update) | async-done | bytes 589840 | tf_op jit(solution)/shard_map/reduce_scatter | solution.py:79
  349.4 2.2 convert_element_type.76
  351.6 2.4 gather_fusion
  354.2 0.6 copy.66
  354.8 161.3 %reduce-scatter.3.cloned.1.call-done = bf16[384,1536]{1,0:T(8,128)(2,1)} async-done(((bf16[3072,1536]{1,0:T(8,128)(2,1)}), bf16[384,1536]{1,0:T(8,128)(2,1)}) %reduce-scatter.3.cloned.1.call-update) | async-done | bytes 1179664 | tf_op jit(solution)/shard_map/reduce_scatter | solution.py:76
  516.1 3.0 bitcast_convert_fusion
  (46 shorter events, 2.4 us)
Async XLA Ops:
  7.2 24.8 %all-gather.4.cloned.1.call-start = ((), (), s32[]{:S(2)}) async-start(), calls=%async_computation.3 | async-start | bytes 1966080 | tf_op jit(solution)/shard_map/all_gather | solution.py:40
  7.9 164.3 %all-gather.6.cloned.1.call-start = ((), (), s32[]{:S(2)}) async-start(), calls=%async_computation.4 | async-start | bytes 10616832 | tf_op jit(solution)/shard_map/all_gather | solution.py:35
  8.6 243.9 %all-gather.8.cloned.1.call-start = ((), (), s32[]{:S(2)}) async-start(), calls=%async_computation.6 | async-start | bytes 5308416 | tf_op jit(solution)/shard_map/all_gather | solution.py:36
  9.4 340.1 %reduce-scatter.5.cloned.1.call-start = ((), (), s32[]{:S(2)}) async-start(), calls=%async_computation.7 | async-start | bytes 5308416 | tf_op jit(solution)/shard_map/reduce_scatter | solution.py:79
  39.3 0.7 copy-start.1
  39.3 12.8 %copy-start.2 = (f32[128,2]{0,1:T(2,128)S(1)}, f32[128,2]{0,1:T(2,128)}, u32[]{:S(2)}) copy-start(f32[128,2]{0,1:T(2,128)} %param.9) | copy-start | bytes 3076
  39.3 26.1 %copy-start = (bf16[512,1536]{1,0:T(8,128)(2,1)S(1)}, bf16[512,1536]{1,0:T(8,128)(2,1)}, u32[]{:S(2)}) copy-start(bf16[512,1536]{1,0:T(8,128)(2,1)} %all-gather.4.cloned.1.call-done) | copy-start | bytes 4718596
  39.3 476.8 %reduce-scatter.3.cloned.1.call-start = ((), (), s32[]{:S(2)}) async-start(), calls=%async_computation.5 | async-start | bytes 10616832 | tf_op jit(solution)/shard_map/reduce_scatter | solution.py:76
  183.0 168.6 %all-to-all-start = ((f32[4,1,96]{2,1,0:T(1,128)}), f32[4,1,96]{2,1,0:T(1,128)S(1)}, u32[]{:S(2)}, u32[]{:S(2)}) async-start(f32[4,1,96]{2,1,0:T(1,128)} %all_to_all.8), calls=%async_computation.2 | async-start | bytes 4096 | tf_op jit(solution)/shard_map/all_to_all | solution.py:62
Sparse Core Ops, SparseCore 0:
  9.6 22.3 all-gather.3
  34.1 138.0 all-gather.5
  174.4 78.0 all-gather.7
  256.0 93.3 reduce-scatter.4
  352.9 163.1 reduce-scatter.2
where the time goes:
time: 526 us
  waiting for transfers between devices  429 us (82%)
  matrix products  35.2 us (7%)
  local copies, waits for them, and re-layouts  21.5 us (4%)
  between operations  13.9 us (3%)
  other arithmetic  11.9 us (2%)
  blocking collectives  10.8 us (2%)
    reduce_scatter x1, waiting for transfers between devices, body(): lax.psum_scatter(routed_term.astype(jnp.bfloat16), 'dp', scatter_dimensio...  161 us
    reduce_scatter x1, waiting for transfers between devices, body(): lax.psum_scatter(shared_term.astype(jnp.bfloat16), 'dp', scatter_dimensio...  89.5 us
    all_gather x1, waiting for transfers between devices, body(): lax.all_gather(routed_down, 'dp', axis=1, tiled=True)  87.2 us
    all_gather x1, waiting for transfers between devices, body(): lax.all_gather(shared_down, 'dp', axis=0, tiled=True)  66.1 us
    all_gather x1, waiting for transfers between devices, body(): lax.all_gather(grad_out, 'expert', axis=0, tiled=True)  22.5 us
  transfers between devices with their start and end apart: 6, of which 5 were waited for; matrix products, arithmetic and copies ran while one was open for 12% of the time, Pallas kernels for 0%

commit v1 on v0

--- a/solution.py
+++ b/solution.py
@@ -1,6 +1,10 @@
+import functools
+
 import jax
 import jax.numpy as jnp
 from jax import lax
+from jax.experimental import pallas as pl
+from jax.experimental.pallas import tpu as pltpu
 from jax.sharding import PartitionSpec as P
 
 SQRT_TWO_PI = 0.7978845608028654
@@ -89,6 +93,315 @@
     )
 
 
+def flip(value, mask, bits):
+    out = 0
+    for bit in range(bits):
+        has = lax.rem(value // (1 << bit), 2)
+        out = out + ((1 - has) if (mask >> bit) & 1 else has) * (1 << bit)
+    return out
+
+
+def flip_by(value, mask, bits):
+    out = 0
+    for bit in range(bits):
+        a, b = lax.rem(value // (1 << bit), 2), lax.rem(mask // (1 << bit), 2)
+        out = out + (a + b - 2 * a * b) * (1 << bit)
+    return out
+
+
+def token_kernel(
+    dp_bits, exp_bits, cap,
+    grad, meta, pre_r, pre_s, down_r, down_s,
+    out_r, out_s, grad_r, grad_s, gate_out,
+    rows, metas, in_r, in_s, stage_r, stage_s, routed, scaled, gate_part, gate_recv, gate_sum, gate_last,
+    ag_send, ag_recv, m1_send, m1_recv, m2_send, m2_recv,
+    inr_send, inr_recv, ins_send, ins_recv, outr_send, outr_recv, outs_send, outs_recv,
+    g1_send, g1_recv, g2_send, g2_recv, local,
+):
+    n_dp, n_exp = 1 << dp_bits, 1 << exp_bits
+    d, e = lax.axis_index("dp"), lax.axis_index("expert")
+    own = d * n_exp + e
+    bits = dp_bits + exp_bits
+    tok = grad.shape[0]
+    hid_r, hid_s = down_r.shape[0], down_s.shape[0]
+    group = n_exp * tok
+
+    def dp_peer(mask):
+        return {"dp": flip(d, mask, dp_bits), "expert": e}
+
+    def exp_peer(mask):
+        return {"dp": d, "expert": flip(e, mask, exp_bits)}
+
+    def peer(bit):
+        return exp_peer(1 << bit) if bit < exp_bits else dp_peer(1 << (bit - exp_bits))
+
+    def remote(source, target, send, recv, device):
+        return pltpu.make_async_remote_copy(
+            src_ref=source, dst_ref=target, send_sem=send, recv_sem=recv,
+            device_id=device, device_id_type=pl.DeviceIdType.MESH,
+        )
+
+    barrier = pltpu.get_barrier_semaphore()
+    for mask in range(1, n_dp):
+        pl.semaphore_signal(barrier, inc=1, device_id=dp_peer(mask), device_id_type=pl.DeviceIdType.MESH)
+    for mask in range(1, n_exp):
+        pl.semaphore_signal(barrier, inc=1, device_id=exp_peer(mask), device_id_type=pl.DeviceIdType.MESH)
+
+    def rows_of(mask):
+        at = pl.multiple_of(flip(own, mask, bits) * tok, tok)
+        return rows.at[pl.ds(at, tok), :]
+
+    rows[pl.ds(pl.multiple_of(own * tok, tok), tok), :] = grad[...]
+    metas[d, e] = meta[...]
+    own_r = pltpu.make_async_copy(
+        pre_r.at[:, pl.ds(pl.multiple_of(d * hid_r, hid_r), hid_r)], in_r.at[0], local.at[0]
+    )
+    own_s = pltpu.make_async_copy(
+        pre_s.at[pl.ds(pl.multiple_of(d * hid_s, hid_s), hid_s), :], in_s.at[0], local.at[1]
+    )
+    own_r.start()
+    own_s.start()
+    pl.semaphore_wait(barrier, n_dp + n_exp - 2)
+
+    def hop(mask, bit):
+        got = mask | (1 << bit)
+        return remote(rows_of(mask), rows_of(mask), ag_send.at[got], ag_recv.at[got], peer(bit))
+
+    def arrived(mask):
+        return remote(rows_of(mask), rows_of(mask), ag_send.at[mask], ag_recv.at[mask], peer(0))
+
+    order = list(range(bits))[::-1]
+    meta_first = [
+        remote(metas.at[d, e], metas.at[d, e], m1_send.at[mask], m1_recv.at[mask], exp_peer(mask))
+        for mask in range(1, n_exp)
+    ]
+    for copy in meta_first:
+        copy.start()
+    for bit in order:
+        hop(0, bit).start()
+    for mask in range(n_dp - 1, 0, -1):
+        to = flip(d, mask, dp_bits)
+        remote(
+            pre_r.at[:, pl.ds(pl.multiple_of(to * hid_r, hid_r), hid_r)],
+            in_r.at[mask], inr_send.at[mask], inr_recv.at[mask], dp_peer(mask),
+        ).start()
+        remote(
+            pre_s.at[pl.ds(pl.multiple_of(to * hid_s, hid_s), hid_s), :],
+            in_s.at[mask], ins_send.at[mask], ins_recv.at[mask], dp_peer(mask),
+        ).start()
+    for mask in range(1, n_exp):
+        came = metas.at[d, flip(e, mask, exp_bits)]
+        remote(came, came, m1_send.at[mask], m1_recv.at[mask], exp_peer(mask)).wait_recv()
+    for mask in range(1, n_dp):
+        remote(metas.at[d], metas.at[d], m2_send.at[mask], m2_recv.at[mask], dp_peer(mask)).start()
+
+    grad_r[...] = jnp.zeros_like(grad_r)
+    grad_s[...] = jnp.zeros_like(grad_s)
+    gate_part[...] = jnp.zeros_like(gate_part)
+
+    held = [0]
+    for place, bit in enumerate(order):
+        fresh = [mask | (1 << bit) for mask in held]
+        for mask in fresh:
+            arrived(mask).wait_recv()
+            for later in order[place + 1:]:
+                hop(mask, later).start()
+        held = held + fresh
+    for mask in range(1, n_dp):
+        came = metas.at[flip(d, mask, dp_bits)]
+        remote(came, came, m2_send.at[mask], m2_recv.at[mask], dp_peer(mask)).wait_recv()
+    own_r.wait()
+    own_s.wait()
+
+    columns = pl.ds(pl.multiple_of(d * hid_r, hid_r), hid_r)
+    lines = pl.ds(pl.multiple_of(d * hid_s, hid_s), hid_s)
+
+    @pl.loop(0, n_dp)
+    def _(turn):
+        mask = n_dp - 1 - turn
+        p = flip_by(d, mask, dp_bits)
+        target = {"dp": p, "expert": e}
+
+        @pl.when(mask > 0)
+        def _():
+            remote(in_r.at[mask], in_r.at[mask], inr_send.at[mask], inr_recv.at[mask], target).wait_recv()
+            remote(in_s.at[mask], in_s.at[mask], ins_send.at[mask], ins_recv.at[mask], target).wait_recv()
+
+        group_rows = rows[pl.ds(pl.multiple_of(p * group, group), group), :]
+        raw_s = lax.dot_general(
+            down_s[...], group_rows, (((1,), (1,)), ((), ())), preferred_element_type=jnp.float32
+        )
+        value_s, slope_s = gelu_pair(in_s[mask].astype(jnp.float32))
+        stage_s[mask] = (raw_s * slope_s).astype(jnp.bfloat16)
+
+        gate_cols = []
+        picks = []
+        line = lax.broadcasted_iota(jnp.int32, (cap, tok), 0).astype(jnp.float32)
+        expert = e.astype(jnp.float32)
+        for s in range(n_exp):
+            info = metas[p, s]
+            pick0 = (info[0:1] == expert) & (info[2:3] == line)
+            pick1 = (info[1:2] == expert) & (info[3:4] == line)
+            gate = info[4:6].astype(jnp.bfloat16).astype(jnp.float32)
+            weight = jnp.where(pick0, gate[0:1], 0.0) + jnp.where(pick1, gate[1:2], 0.0)
+            chosen = (jnp.where(pick0, 1.0, 0.0) + jnp.where(pick1, 1.0, 0.0)).astype(jnp.bfloat16)
+            block = lax.dot_general(
+                chosen, group_rows[s * tok:(s + 1) * tok], (((1,), (0,)), ((), ())),
+                preferred_element_type=jnp.float32,
+            )
+            gate_col = jnp.sum(weight, axis=1, keepdims=True)
+            routed[s * cap:(s + 1) * cap, :] = block.astype(jnp.bfloat16)
+            scaled[s * cap:(s + 1) * cap, :] = (gate_col * block).astype(jnp.bfloat16)
+            gate_cols.append(gate_col)
+            picks.append((pick0, pick1))
+        raw = lax.dot_general(
+            routed[...], down_r[...], (((1,), (1,)), ((), ())), preferred_element_type=jnp.float32
+        )
+        value, slope = gelu_pair(in_r[mask].astype(jnp.float32))
+        stage_r[mask] = (jnp.concatenate(gate_cols, axis=0) * raw * slope).astype(jnp.bfloat16)
+        score = jnp.sum(value * raw, axis=1, keepdims=True)
+        for s in range(n_exp):
+            part = score[s * cap:(s + 1) * cap]
+            for k in range(2):
+                gate_part[mask, s, k:k + 1, :] = jnp.sum(
+                    jnp.where(picks[s][k], part, 0.0), axis=0, keepdims=True
+                )
+
+        @pl.when(mask > 0)
+        def _():
+            remote(stage_r.at[mask], out_r.at[:, columns], outr_send.at[mask], outr_recv.at[mask], target).start()
+            remote(stage_s.at[mask], out_s.at[lines, :], outs_send.at[mask], outs_recv.at[mask], target).start()
+            remote(gate_part.at[mask], gate_recv.at[mask], g1_send.at[mask], g1_recv.at[mask], target).start()
+
+        grad_s[...] += lax.dot_general(
+            value_s.astype(jnp.bfloat16), group_rows, (((1,), (0,)), ((), ())), preferred_element_type=jnp.float32
+        )
+        grad_r[...] += lax.dot_general(
+            value.astype(jnp.bfloat16), scaled[...], (((0,), (0,)), ((), ())), preferred_element_type=jnp.float32
+        )
+
+    last_r = pltpu.make_async_copy(stage_r.at[0], out_r.at[:, columns], local.at[2])
+    last_s = pltpu.make_async_copy(stage_s.at[0], out_s.at[lines, :], local.at[3])
+    last_r.start()
+    last_s.start()
+
+    total = gate_part[0]
+    for mask in range(1, n_dp):
+        remote(
+            gate_recv.at[mask], gate_recv.at[mask], g1_send.at[mask], g1_recv.at[mask], dp_peer(mask)
+        ).wait_recv()
+        total = total + gate_recv[mask]
+    gate_sum[...] = total
+    for mask in range(1, n_exp):
+        remote(
+            gate_sum.at[flip(e, mask, exp_bits)], gate_last.at[mask], g2_send.at[mask], g2_recv.at[mask], exp_peer(mask)
+        ).start()
+    final = gate_sum[e]
+    for mask in range(1, n_exp):
+        remote(
+            gate_last.at[mask], gate_last.at[mask], g2_send.at[mask], g2_recv.at[mask], exp_peer(mask)
+        ).wait_recv()
+        final = final + gate_last[mask]
+    gate_out[...] = final
+
+    for mask in range(1, n_dp):
+        origin = flip(d, mask, dp_bits)
+        from_r = out_r.at[:, pl.ds(pl.multiple_of(origin * hid_r, hid_r), hid_r)]
+        from_s = out_s.at[pl.ds(pl.multiple_of(origin * hid_s, hid_s), hid_s), :]
+        remote(stage_r.at[mask], from_r, outr_send.at[mask], outr_recv.at[mask], dp_peer(mask)).wait()
+        remote(stage_s.at[mask], from_s, outs_send.at[mask], outs_recv.at[mask], dp_peer(mask)).wait()
+        remote(in_r.at[mask], in_r.at[mask], inr_send.at[mask], inr_recv.at[mask], dp_peer(mask)).wait_send()
+        remote(in_s.at[mask], in_s.at[mask], ins_send.at[mask], ins_recv.at[mask], dp_peer(mask)).wait_send()
+        remote(metas.at[d], metas.at[d], m2_send.at[mask], m2_recv.at[mask], dp_peer(mask)).wait_send()
+        remote(
+            gate_part.at[mask], gate_recv.at[mask], g1_send.at[mask], g1_recv.at[mask], dp_peer(mask)
+        ).wait_send()
+    for mask in range(1, n_exp):
+        remote(metas.at[d, e], metas.at[d, e], m1_send.at[mask], m1_recv.at[mask], exp_peer(mask)).wait_send()
+        remote(
+            gate_sum.at[flip(e, mask, exp_bits)], gate_last.at[mask], g2_send.at[mask], g2_recv.at[mask], exp_peer(mask)
+        ).wait_send()
+    for mask in range(1, n_dp * n_exp):
+        arrived(mask).wait_send()
+    last_r.wait()
+    last_s.wait()
+
+
+def token_body(grad_out, expert_ids, gates, routed_pre, routed_down, shared_pre, shared_down):
+    n_dp, n_exp = lax.axis_size("dp"), lax.axis_size("expert")
+    dp_bits, exp_bits = n_dp.bit_length() - 1, n_exp.bit_length() - 1
+    tok, width = grad_out.shape
+    slots, hidden = routed_pre.shape[2:]
+    cap = slots // n_exp
+    hid_r, hid_s = routed_down.shape[1], shared_down.shape[0]
+    group, shared_hidden = shared_pre.shape
+    flat = expert_ids.reshape(tok * 2)
+    place = jnp.arange(tok * 2, dtype=jnp.int32)
+    rank = jnp.sum(
+        ((flat[None, :] == flat[:, None]) & (place[None, :] < place[:, None])).astype(jnp.float32), axis=1
+    ).reshape(tok, 2)
+    meta = jnp.concatenate(
+        [expert_ids.astype(jnp.float32).T, rank.T, gates.T, jnp.zeros((2, tok), jnp.float32)], axis=0
+    )
+    any_spec, vmem = pl.BlockSpec(memory_space=pl.ANY), pl.BlockSpec(memory_space=pltpu.VMEM)
+    bf, f32, dma = jnp.bfloat16, jnp.float32, pltpu.SemaphoreType.DMA
+    every = n_dp * n_exp
+    flops = 4 * n_dp * width * (slots * hid_r + group * hid_s)
+    out_r, out_s, grad_r, grad_s, gate = pl.pallas_call(
+        functools.partial(token_kernel, dp_bits, exp_bits, cap),
+        out_shape=[
+            jax.ShapeDtypeStruct((slots, hidden), bf),
+            jax.ShapeDtypeStruct((shared_hidden, group), bf),
+            jax.ShapeDtypeStruct((hid_r, width), f32),
+            jax.ShapeDtypeStruct((hid_s, width), f32),
+            jax.ShapeDtypeStruct((8, tok), f32),
+        ],
+        in_specs=[vmem, vmem, any_spec, any_spec, vmem, vmem],
+        out_specs=[any_spec, any_spec, vmem, vmem, vmem],
+        scratch_shapes=[
+            pltpu.VMEM((every * tok, width), bf),
+            pltpu.VMEM((n_dp, n_exp, 8, tok), f32),
+            pltpu.VMEM((n_dp, slots, hid_r), bf),
+            pltpu.VMEM((n_dp, hid_s, group), bf),
+            pltpu.VMEM((n_dp, slots, hid_r), bf),
+            pltpu.VMEM((n_dp, hid_s, group), bf),
+            pltpu.VMEM((slots, width), bf),
+            pltpu.VMEM((slots, width), bf),
+            pltpu.VMEM((n_dp, n_exp, 8, tok), f32),
+            pltpu.VMEM((n_dp, n_exp, 8, tok), f32),
+            pltpu.VMEM((n_exp, 8, tok), f32),
+            pltpu.VMEM((n_exp, 8, tok), f32),
+            dma((every,)), dma((every,)),
+            dma((n_exp,)), dma((n_exp,)),
+            dma((n_dp,)), dma((n_dp,)),
+            dma((n_dp,)), dma((n_dp,)), dma((n_dp,)), dma((n_dp,)),
+            dma((n_dp,)), dma((n_dp,)), dma((n_dp,)), dma((n_dp,)),
+            dma((n_dp,)), dma((n_dp,)),
+            dma((n_exp,)), dma((n_exp,)),
+            dma((4,)),
+        ],
+        compiler_params=pltpu.CompilerParams(
+            collective_id=0, has_side_effects=True, vmem_limit_bytes=56 << 20
+        ),
+        cost_estimate=pl.CostEstimate(flops=flops, bytes_accessed=16 << 20, transcendentals=0),
+    )(grad_out, meta, routed_pre[0, 0], shared_pre.T, routed_down[0], shared_down)
+    return (
+        out_r.reshape(routed_pre.shape),
+        grad_r[None],
+        out_s.T,
+        grad_s,
+        gate[:2].T,
+    )
+
+
+def by_tokens(mesh, shapes):
+    n_dp, n_exp = mesh.shape["dp"], mesh.shape["expert"]
+    tokens, (hidden, shared) = shapes[0][0], (shapes[4][1], shapes[6][0])
+    powers = n_dp & (n_dp - 1) == 0 and n_exp & (n_exp - 1) == 0
+    aligned = hidden % (128 * n_dp) == 0 and shared % (16 * n_dp * n_exp) == 0
+    return powers and aligned and tokens <= hidden + shared // n_exp
+
+
 def solution(mesh):
     in_specs = (
         P(("dp", "expert"), None),
@@ -106,4 +419,11 @@
         P(("expert", "dp"), None),
         P(("dp", "expert"), None),
     )
-    return jax.shard_map(body, mesh=mesh, in_specs=in_specs, out_specs=out_specs, check_vma=False)
+
+    def run(*args):
+        chosen = token_body if by_tokens(mesh, [a.shape for a in args]) else body
+        return jax.shard_map(
+            chosen, mesh=mesh, in_specs=in_specs, out_specs=out_specs, check_vma=False
+        )(*args)
+
+    return run

time: 526 us -> 246 us (0.47)
  waiting for transfers between devices: 429 us -> 0 us
  Pallas kernels: 0 us -> 229 us
  matrix products: 35.2 us -> 0 us
  between operations: 13.9 us -> 0.67 us
  blocking collectives: 10.8 us -> 0 us
  other arithmetic: 11.9 us -> 2.23 us
  local copies, waits for them, and re-layouts: 21.5 us -> 13.4 us
    reduce_scatter x2 -> x0, waiting for transfers between devices: 251 us -> none  [the longest x1 161 us: body(): lax.psum_scatter(routed_term.astype(jnp.bfloat16), 'dp', scatter_dimensio...]
    pallas_call x0 -> x1, Pallas kernels: none -> 229 us  [token_body(): pl.pallas_call(functools.partial(token_kernel, dp_bits, exp_bits, cap), o...]
    all_gather x3 -> x0, waiting for transfers between devices: 176 us -> none  [the longest x1 87.2 us: body(): lax.all_gather(routed_down, 'dp', axis=1, tiled=True)]
    dot_general x4 -> x0, matrix products: 35.2 us -> none  [the longest x1 10.3 us: body(): lax.dot_general(hidden_b, scaled, (((0,), (0,)), ((), ())), preferred_ele...]
    scatter x3 -> x0, local copies, waits for them, and re-layouts: 14.5 us -> none  [the longest x1 7.58 us: body(): jnp.zeros((slots + 1,), jnp.bfloat16).at[target].set(group_gate)[:slots]]
    all_gather x2 -> x0, blocking collectives: 10.8 us -> none  [the longest x1 5.78 us: body(): group_ids = lax.all_gather(expert_ids, 'expert', axis=0, tiled=True)]
    unnamed x8 -> x12, local copies, waits for them, and re-layouts: 1.36 us -> 11.7 us
    another operation x6 -> x0, other arithmetic: 6.2 us -> none
  transfers between devices with their start and end apart: 6 -> 0, of which waited for: 5 -> 0; matrix products, arithmetic and copies ran while one was open for 12% -> 0% of each run, Pallas kernels for 0% -> 0%
where the time goes in v1:
time: 246 us; the launch traced here: 245 us
  Pallas kernels  229 us (93%)
  local copies, waits for them, and re-layouts  13.4 us (5%)
    pallas_call x1, Pallas kernels, token_body(): pl.pallas_call(functools.partial(token_kernel, dp_bits, exp_bits, cap), o...  229 us
    unnamed x12, local copies, waits for them, and re-layouts  11.7 us

profile of v1, /device:TPU:0, one launch (start us, length us, event | category | flops | bytes accessed | tf_op | source)
XLA Modules:
  0.0 245.4 jit_solution(16819148190945861600)
XLA Ops:
  0.6 0.1 pad.3.clone
  0.7 0.7 convert_bitcast_fusion
  1.4 0.8 copy.18
  2.2 0.1 eq.15
  2.3 0.2 convert_reduce_fusion
  2.5 0.1 reshape.18
  2.7 0.1 copy.19
  2.7 1.4 maximum_maximum_fusion.meta
  4.1 2.6 %copy.20 = bf16[512,1536]{0,1:T(8,128)(2,1)} copy(bf16[512,1536]{1,0:T(8,128)(2,1)} %param.12) | data formatting | bytes 3145728 | tf_op args[5]
  6.7 229.1 %shard_map.110 = (bf16[384,3072]{1,0:T(8,128)(2,1)}, bf16[1536,512]{1,0:T(8,128)(2,1)}, f32[384,1536]{1,0:T(8,128)}, f32[192,1536]{1,0:T(8,128)}, f32[8,128]{1,0:T(8,128)}) custom-call(bf16[128,1536]{1,0:T(8,128)(2,1)} %grad.1, f32[8,128]{1,0:T(8,128)} %maximum_maximum_fusion.meta, bf16[384,3072]{1,0:T(8,128)(2,1)} %bitcast.18, bf16[1536,512]{1,0:T(8,128)(2,1)} %bitcast.15, ...), custom_call_target="tpu_custom_call" | custom-call | flops 12079595520 | bytes 16777216 | tf_op jit(solution)/shard_map/pallas_call | solution.py:350
  235.8 1.2 slice_bitcast_fusion
  237.1 0.0 copy-start.1
  237.1 2.7 %copy.21 = bf16[512,1536]{1,0:T(8,128)(2,1)} copy(bf16[512,1536]{0,1:T(8,128)(2,1)} %bitcast.14) | data formatting | bytes 3145728
  239.8 0.0 copy-done.1
  239.8 0.0 copy-start
  239.8 1.4 copy.25
  241.2 1.1 copy-done
  242.3 0.0 copy-start.2
  242.3 1.4 copy.26
  243.7 0.7 copy-done.2
  244.4 1.0 copy.27
  (1 shorter events, 0.0 us)
Async XLA Ops:
  237.1 2.7 %copy-start.1 = (bf16[384,3072]{1,0:T(8,128)(2,1)S(1)}, bf16[384,3072]{1,0:T(8,128)(2,1)}, u32[]{:S(2)}) copy-start(bf16[384,3072]{1,0:T(8,128)(2,1)} %get-tuple-element.10) | copy-start | bytes 7077892
  239.8 2.5 %copy-start = (f32[384,1536]{1,0:T(8,128)S(1)}, f32[384,1536]{1,0:T(8,128)}, u32[]{:S(2)}) copy-start(f32[384,1536]{1,0:T(8,128)} %get-tuple-element.11) | copy-start | bytes 7077892
  242.3 2.1 copy-start.2

commit v2 on v1

--- a/solution.py
+++ b/solution.py
@@ -179,7 +179,8 @@
         copy.start()
     for bit in order:
         hop(0, bit).start()
-    for mask in range(n_dp - 1, 0, -1):
+
+    def give(mask):
         to = flip(d, mask, dp_bits)
         remote(
             pre_r.at[:, pl.ds(pl.multiple_of(to * hid_r, hid_r), hid_r)],
@@ -189,6 +190,7 @@
             pre_s.at[pl.ds(pl.multiple_of(to * hid_s, hid_s), hid_s), :],
             in_s.at[mask], ins_send.at[mask], ins_recv.at[mask], dp_peer(mask),
         ).start()
+
     for mask in range(1, n_exp):
         came = metas.at[d, flip(e, mask, exp_bits)]
         remote(came, came, m1_send.at[mask], m1_recv.at[mask], exp_peer(mask)).wait_recv()
@@ -207,6 +209,12 @@
             for later in order[place + 1:]:
                 hop(mask, later).start()
         held = held + fresh
+        if bit == exp_bits + 1:
+            for mask in range(n_dp - 2, 0, -2):
+                give(mask)
+        if bit == exp_bits:
+            for mask in range(n_dp - 1, 0, -2):
+                give(mask)
     for mask in range(1, n_dp):
         came = metas.at[flip(d, mask, dp_bits)]
         remote(came, came, m2_send.at[mask], m2_recv.at[mask], dp_peer(mask)).wait_recv()
@@ -219,6 +227,9 @@
     @pl.loop(0, n_dp)
     def _(turn):
         mask = n_dp - 1 - turn
+        if dp_bits == 3:
+            high, middle, low = turn // 4, lax.rem(turn // 2, 2), lax.rem(turn, 2)
+            mask = 4 * (1 - high) + 2 * (1 - low) + middle
         p = flip_by(d, mask, dp_bits)
         target = {"dp": p, "expert": e}
 

time: 246 us -> 235 us (0.955)
  Pallas kernels: 229 us -> 216 us
    pallas_call x1, Pallas kernels: 229 us -> 216 us  [token_body(): pl.pallas_call(functools.partial(token_kernel, dp_bits, exp_bits, cap), o...]
where the time goes in v2:
time: 235 us; the launch traced here: 232 us
  Pallas kernels  216 us (92%)
  local copies, waits for them, and re-layouts  13.4 us (6%)
    pallas_call x1, Pallas kernels, token_body(): pl.pallas_call(functools.partial(token_kernel, dp_bits, exp_bits, cap), o...  216 us
    unnamed x12, local copies, waits for them, and re-layouts  11.7 us

profile of v2, /device:TPU:0, one launch (start us, length us, event | category | flops | bytes accessed | tf_op | source)
XLA Modules:
  0.0 232.2 jit_solution(18402287605544862579)
XLA Ops:
  0.6 0.1 pad.3.clone
  0.7 0.7 convert_bitcast_fusion
  1.4 0.8 copy.18
  2.2 0.1 eq.15
  2.3 0.2 convert_reduce_fusion
  2.5 0.1 reshape.18
  2.7 0.1 copy.19
  2.7 1.4 maximum_maximum_fusion.meta
  4.1 2.6 %copy.20 = bf16[512,1536]{0,1:T(8,128)(2,1)} copy(bf16[512,1536]{1,0:T(8,128)(2,1)} %param.12) | data formatting | bytes 3145728 | tf_op args[5]
  6.7 215.9 %shard_map.110 = (bf16[384,3072]{1,0:T(8,128)(2,1)}, bf16[1536,512]{1,0:T(8,128)(2,1)}, f32[384,1536]{1,0:T(8,128)}, f32[192,1536]{1,0:T(8,128)}, f32[8,128]{1,0:T(8,128)}) custom-call(bf16[128,1536]{1,0:T(8,128)(2,1)} %grad.1, f32[8,128]{1,0:T(8,128)} %maximum_maximum_fusion.meta, bf16[384,3072]{1,0:T(8,128)(2,1)} %bitcast.18, bf16[1536,512]{1,0:T(8,128)(2,1)} %bitcast.15, ...), custom_call_target="tpu_custom_call" | custom-call | flops 12079595520 | bytes 16777216 | tf_op jit(solution)/shard_map/pallas_call | solution.py:361
  222.6 1.2 slice_bitcast_fusion
  223.8 0.0 copy-start.1
  223.8 2.7 %copy.21 = bf16[512,1536]{1,0:T(8,128)(2,1)} copy(bf16[512,1536]{0,1:T(8,128)(2,1)} %bitcast.14) | data formatting | bytes 3145728
  226.6 0.0 copy-done.1
  226.6 0.0 copy-start
  226.6 1.4 copy.25
  228.0 1.1 copy-done
  229.1 0.0 copy-start.2
  229.1 1.4 copy.26
  230.5 0.7 copy-done.2
  231.2 1.0 copy.27
  (1 shorter events, 0.0 us)
Async XLA Ops:
  223.8 2.7 %copy-start.1 = (bf16[384,3072]{1,0:T(8,128)(2,1)S(1)}, bf16[384,3072]{1,0:T(8,128)(2,1)}, u32[]{:S(2)}) copy-start(bf16[384,3072]{1,0:T(8,128)(2,1)} %get-tuple-element.10) | copy-start | bytes 7077892
  226.6 2.5 %copy-start = (f32[384,1536]{1,0:T(8,128)S(1)}, f32[384,1536]{1,0:T(8,128)}, u32[]{:S(2)}) copy-start(f32[384,1536]{1,0:T(8,128)} %get-tuple-element.11) | copy-start | bytes 7077892
  229.1 2.1 copy-start.2

commit v3 on v1

--- a/solution.py
+++ b/solution.py
@@ -113,15 +113,20 @@
     dp_bits, exp_bits, cap,
     grad, meta, pre_r, pre_s, down_r, down_s,
     out_r, out_s, grad_r, grad_s, gate_out,
-    rows, metas, in_r, in_s, stage_r, stage_s, routed, scaled, gate_part, gate_recv, gate_sum, gate_last,
+    rows, metas, in_r, in_s, stage_r, stage_s, routed, scaled,
+    weight_r, weight_s, far_r, far_s, sent_r, sent_s, got_r, got_s,
+    gate_part, gate_recv, gate_sum, gate_last,
     ag_send, ag_recv, m1_send, m1_recv, m2_send, m2_recv,
     inr_send, inr_recv, ins_send, ins_recv, outr_send, outr_recv, outs_send, outs_recv,
-    g1_send, g1_recv, g2_send, g2_recv, local,
+    g1_send, g1_recv, g2_send, g2_recv, pair_send, pair_recv, local,
 ):
-    n_dp, n_exp = 1 << dp_bits, 1 << exp_bits
+    n_exp, low_bits = 1 << exp_bits, dp_bits - 1
+    n_low = 1 << low_bits
     d, e = lax.axis_index("dp"), lax.axis_index("expert")
-    own = d * n_exp + e
-    bits = dp_bits + exp_bits
+    low = lax.rem(d, n_low)
+    base = d - low
+    own = low * n_exp + e
+    bits = low_bits + exp_bits
     tok = grad.shape[0]
     hid_r, hid_s = down_r.shape[0], down_s.shape[0]
     group = n_exp * tok
@@ -141,27 +146,34 @@
             device_id=device, device_id_type=pl.DeviceIdType.MESH,
         )
 
+    def columns(at):
+        return pl.ds(pl.multiple_of(at * hid_r, hid_r), hid_r)
+
+    def lines(at):
+        return pl.ds(pl.multiple_of(at * hid_s, hid_s), hid_s)
+
+    def side_of(value, side):
+        return flip(value, side * n_low, dp_bits)
+
     barrier = pltpu.get_barrier_semaphore()
-    for mask in range(1, n_dp):
-        pl.semaphore_signal(barrier, inc=1, device_id=dp_peer(mask), device_id_type=pl.DeviceIdType.MESH)
-    for mask in range(1, n_exp):
-        pl.semaphore_signal(barrier, inc=1, device_id=exp_peer(mask), device_id_type=pl.DeviceIdType.MESH)
+    partners = [dp_peer(mask) for mask in range(1, n_low + 1)] + [exp_peer(mask) for mask in range(1, n_exp)]
+    for device in partners:
+        pl.semaphore_signal(barrier, inc=1, device_id=device, device_id_type=pl.DeviceIdType.MESH)
 
     def rows_of(mask):
         at = pl.multiple_of(flip(own, mask, bits) * tok, tok)
         return rows.at[pl.ds(at, tok), :]
 
     rows[pl.ds(pl.multiple_of(own * tok, tok), tok), :] = grad[...]
-    metas[d, e] = meta[...]
-    own_r = pltpu.make_async_copy(
-        pre_r.at[:, pl.ds(pl.multiple_of(d * hid_r, hid_r), hid_r)], in_r.at[0], local.at[0]
-    )
-    own_s = pltpu.make_async_copy(
-        pre_s.at[pl.ds(pl.multiple_of(d * hid_s, hid_s), hid_s), :], in_s.at[0], local.at[1]
-    )
-    own_r.start()
-    own_s.start()
-    pl.semaphore_wait(barrier, n_dp + n_exp - 2)
+    metas[low, e] = meta[...]
+    locals_in = []
+    for side in range(2):
+        at = side_of(d, side)
+        locals_in.append(pltpu.make_async_copy(pre_r.at[:, columns(at)], in_r.at[side], local.at[2 * side]))
+        locals_in.append(pltpu.make_async_copy(pre_s.at[lines(at), :], in_s.at[side], local.at[2 * side + 1]))
+    for copy in locals_in:
+        copy.start()
+    pl.semaphore_wait(barrier, len(partners))
 
     def hop(mask, bit):
         got = mask | (1 << bit)
@@ -170,34 +182,38 @@
     def arrived(mask):
         return remote(rows_of(mask), rows_of(mask), ag_send.at[mask], ag_recv.at[mask], peer(0))
 
+    def give(mask):
+        for side in (1, 0):
+            at = side_of(flip(d, mask, dp_bits), side)
+            slot = 2 * mask + side
+            remote(
+                pre_r.at[:, columns(at)], in_r.at[slot], inr_send.at[slot], inr_recv.at[slot], dp_peer(mask)
+            ).start()
+            remote(
+                pre_s.at[lines(at), :], in_s.at[slot], ins_send.at[slot], ins_recv.at[slot], dp_peer(mask)
+            ).start()
+
+    def pair(source, target, index):
+        return remote(source, target, pair_send.at[index], pair_recv.at[index], dp_peer(n_low))
+
     order = list(range(bits))[::-1]
-    meta_first = [
-        remote(metas.at[d, e], metas.at[d, e], m1_send.at[mask], m1_recv.at[mask], exp_peer(mask))
-        for mask in range(1, n_exp)
-    ]
-    for copy in meta_first:
-        copy.start()
+    for mask in range(1, n_exp):
+        remote(metas.at[low, e], metas.at[low, e], m1_send.at[mask], m1_recv.at[mask], exp_peer(mask)).start()
     for bit in order:
         hop(0, bit).start()
-    for mask in range(n_dp - 1, 0, -1):
-        to = flip(d, mask, dp_bits)
-        remote(
-            pre_r.at[:, pl.ds(pl.multiple_of(to * hid_r, hid_r), hid_r)],
-            in_r.at[mask], inr_send.at[mask], inr_recv.at[mask], dp_peer(mask),
-        ).start()
-        remote(
-            pre_s.at[pl.ds(pl.multiple_of(to * hid_s, hid_s), hid_s), :],
-            in_s.at[mask], ins_send.at[mask], ins_recv.at[mask], dp_peer(mask),
-        ).start()
+    weights = [pair(down_s, weight_s.at[1], 1), pair(down_r, weight_r.at[1], 0)]
+    for copy in weights:
+        copy.start()
     for mask in range(1, n_exp):
-        came = metas.at[d, flip(e, mask, exp_bits)]
+        came = metas.at[low, flip(e, mask, exp_bits)]
         remote(came, came, m1_send.at[mask], m1_recv.at[mask], exp_peer(mask)).wait_recv()
-    for mask in range(1, n_dp):
-        remote(metas.at[d], metas.at[d], m2_send.at[mask], m2_recv.at[mask], dp_peer(mask)).start()
-
-    grad_r[...] = jnp.zeros_like(grad_r)
-    grad_s[...] = jnp.zeros_like(grad_s)
-    gate_part[...] = jnp.zeros_like(gate_part)
+    for mask in range(1, n_low):
+        remote(metas.at[low], metas.at[low], m2_send.at[mask], m2_recv.at[mask], dp_peer(mask)).start()
+
+    for ref in (grad_r, grad_s, far_r, far_s, gate_part):
+        ref[...] = jnp.zeros_like(ref)
+    weight_r[0] = down_r[...]
+    weight_s[0] = down_s[...]
 
     held = [0]
     for place, bit in enumerate(order):
@@ -207,86 +223,128 @@
             for later in order[place + 1:]:
                 hop(mask, later).start()
         held = held + fresh
-    for mask in range(1, n_dp):
-        came = metas.at[flip(d, mask, dp_bits)]
+        if bit == exp_bits + 1:
+            for mask in range(n_low - 2, 0, -2):
+                give(mask)
+        if bit == exp_bits:
+            for mask in range(n_low - 1, 0, -2):
+                give(mask)
+    for mask in range(1, n_low):
+        came = metas.at[flip(low, mask, low_bits)]
         remote(came, came, m2_send.at[mask], m2_recv.at[mask], dp_peer(mask)).wait_recv()
-    own_r.wait()
-    own_s.wait()
-
-    columns = pl.ds(pl.multiple_of(d * hid_r, hid_r), hid_r)
-    lines = pl.ds(pl.multiple_of(d * hid_s, hid_s), hid_s)
-
-    @pl.loop(0, n_dp)
-    def _(turn):
-        mask = n_dp - 1 - turn
-        p = flip_by(d, mask, dp_bits)
-        target = {"dp": p, "expert": e}
+    for copy in locals_in:
+        copy.wait()
+
+    line = lax.broadcasted_iota(jnp.int32, (cap, tok), 0).astype(jnp.float32)
+    expert = e.astype(jnp.float32)
+
+    def picked(place, s):
+        info = metas[place, s]
+        pick0 = (info[0:1] == expert) & (info[2:3] == line)
+        pick1 = (info[1:2] == expert) & (info[3:4] == line)
+        gate = info[4:6].astype(jnp.bfloat16).astype(jnp.float32)
+        weight = jnp.where(pick0, gate[0:1], 0.0) + jnp.where(pick1, gate[1:2], 0.0)
+        return pick0, pick1, jnp.sum(weight, axis=1, keepdims=True)
+
+    @pl.loop(0, n_low)
+    def _(mask):
+        place = flip_by(low, mask, low_bits)
+        device = {"dp": base + place, "expert": e}
 
         @pl.when(mask > 0)
         def _():
-            remote(in_r.at[mask], in_r.at[mask], inr_send.at[mask], inr_recv.at[mask], target).wait_recv()
-            remote(in_s.at[mask], in_s.at[mask], ins_send.at[mask], ins_recv.at[mask], target).wait_recv()
-
-        group_rows = rows[pl.ds(pl.multiple_of(p * group, group), group), :]
-        raw_s = lax.dot_general(
-            down_s[...], group_rows, (((1,), (1,)), ((), ())), preferred_element_type=jnp.float32
-        )
-        value_s, slope_s = gelu_pair(in_s[mask].astype(jnp.float32))
-        stage_s[mask] = (raw_s * slope_s).astype(jnp.bfloat16)
-
-        gate_cols = []
-        picks = []
-        line = lax.broadcasted_iota(jnp.int32, (cap, tok), 0).astype(jnp.float32)
-        expert = e.astype(jnp.float32)
+            for side in range(2):
+                slot = 2 * mask + side
+                remote(in_r.at[slot], in_r.at[slot], inr_send.at[slot], inr_recv.at[slot], device).wait_recv()
+                remote(in_s.at[slot], in_s.at[slot], ins_send.at[slot], ins_recv.at[slot], device).wait_recv()
+
+        group_rows = rows[pl.ds(pl.multiple_of(place * group, group), group), :]
         for s in range(n_exp):
-            info = metas[p, s]
-            pick0 = (info[0:1] == expert) & (info[2:3] == line)
-            pick1 = (info[1:2] == expert) & (info[3:4] == line)
-            gate = info[4:6].astype(jnp.bfloat16).astype(jnp.float32)
-            weight = jnp.where(pick0, gate[0:1], 0.0) + jnp.where(pick1, gate[1:2], 0.0)
+            pick0, pick1, gate_col = picked(place, s)
             chosen = (jnp.where(pick0, 1.0, 0.0) + jnp.where(pick1, 1.0, 0.0)).astype(jnp.bfloat16)
             block = lax.dot_general(
                 chosen, group_rows[s * tok:(s + 1) * tok], (((1,), (0,)), ((), ())),
                 preferred_element_type=jnp.float32,
             )
-            gate_col = jnp.sum(weight, axis=1, keepdims=True)
-            routed[s * cap:(s + 1) * cap, :] = block.astype(jnp.bfloat16)
+            routed[mask, s * cap:(s + 1) * cap, :] = block.astype(jnp.bfloat16)
             scaled[s * cap:(s + 1) * cap, :] = (gate_col * block).astype(jnp.bfloat16)
-            gate_cols.append(gate_col)
-            picks.append((pick0, pick1))
+        for side, (sum_r, sum_s) in ((1, (far_r, far_s)), (0, (grad_r, grad_s))):
+            value_s, _ = gelu_pair(in_s[2 * mask + side].astype(jnp.float32))
+            sum_s[...] += lax.dot_general(
+                value_s.astype(jnp.bfloat16), group_rows, (((1,), (0,)), ((), ())),
+                preferred_element_type=jnp.float32,
+            )
+            value_r, _ = gelu_pair(in_r[2 * mask + side].astype(jnp.float32))
+            sum_r[...] += lax.dot_general(
+                value_r.astype(jnp.bfloat16), scaled[...], (((0,), (0,)), ((), ())),
+                preferred_element_type=jnp.float32,
+            )
+
+    sent_r[...] = far_r[...].astype(jnp.bfloat16)
+    sent_s[...] = far_s[...].astype(jnp.bfloat16)
+    sums = [pair(sent_r, got_r, 2), pair(sent_s, got_s, 3)]
+    for copy in sums:
+        copy.start()
+
+    @pl.loop(0, 2 * n_low)
+    def _(turn):
+        side = turn // n_low
+        mask = n_low - 1 - lax.rem(turn, n_low)
+        slot = 2 * mask + side
+        place = flip_by(low, mask, low_bits)
+        device = {"dp": base + place, "expert": e}
+        at = lax.rem(d + side * n_low, 2 * n_low)
+
+        @pl.when(turn == n_low)
+        def _():
+            for copy in weights:
+                copy.wait_recv()
+
+        group_rows = rows[pl.ds(pl.multiple_of(place * group, group), group), :]
+        raw_s = lax.dot_general(
+            weight_s[side], group_rows, (((1,), (1,)), ((), ())), preferred_element_type=jnp.float32
+        )
+        _, slope_s = gelu_pair(in_s[slot].astype(jnp.float32))
+        stage_s[slot] = (raw_s * slope_s).astype(jnp.bfloat16)
         raw = lax.dot_general(
-            routed[...], down_r[...], (((1,), (1,)), ((), ())), preferred_element_type=jnp.float32
+            routed[mask], weight_r[side], (((1,), (1,)), ((), ())), preferred_element_type=jnp.float32
         )
-        value, slope = gelu_pair(in_r[mask].astype(jnp.float32))
-        stage_r[mask] = (jnp.concatenate(gate_cols, axis=0) * raw * slope).astype(jnp.bfloat16)
+        value, slope = gelu_pair(in_r[slot].astype(jnp.float32))
+        picks = [picked(place, s) for s in range(n_exp)]
+        gate_col = jnp.concatenate([pick[2] for pick in picks], axis=0)
+        stage_r[slot] = (gate_col * raw * slope).astype(jnp.bfloat16)
+
+        @pl.when(mask > 0)
+        def _():
+            remote(
+                stage_r.at[slot], out_r.at[:, columns(at)], outr_send.at[slot], outr_recv.at[slot], device
+            ).start()
+            remote(
+                stage_s.at[slot], out_s.at[lines(at), :], outs_send.at[slot], outs_recv.at[slot], device
+            ).start()
+
         score = jnp.sum(value * raw, axis=1, keepdims=True)
         for s in range(n_exp):
             part = score[s * cap:(s + 1) * cap]
             for k in range(2):
-                gate_part[mask, s, k:k + 1, :] = jnp.sum(
+                gate_part[mask, s, k:k + 1, :] += jnp.sum(
                     jnp.where(picks[s][k], part, 0.0), axis=0, keepdims=True
                 )
 
-        @pl.when(mask > 0)
+        @pl.when((mask > 0) & (side == 1))
         def _():
-            remote(stage_r.at[mask], out_r.at[:, columns], outr_send.at[mask], outr_recv.at[mask], target).start()
-            remote(stage_s.at[mask], out_s.at[lines, :], outs_send.at[mask], outs_recv.at[mask], target).start()
-            remote(gate_part.at[mask], gate_recv.at[mask], g1_send.at[mask], g1_recv.at[mask], target).start()
-
-        grad_s[...] += lax.dot_general(
-            value_s.astype(jnp.bfloat16), group_rows, (((1,), (0,)), ((), ())), preferred_element_type=jnp.float32
-        )
-        grad_r[...] += lax.dot_general(
-            value.astype(jnp.bfloat16), scaled[...], (((0,), (0,)), ((), ())), preferred_element_type=jnp.float32
-        )
-
-    last_r = pltpu.make_async_copy(stage_r.at[0], out_r.at[:, columns], local.at[2])
-    last_s = pltpu.make_async_copy(stage_s.at[0], out_s.at[lines, :], local.at[3])
-    last_r.start()
-    last_s.start()
+            remote(gate_part.at[mask], gate_recv.at[mask], g1_send.at[mask], g1_recv.at[mask], device).start()
+
+    locals_out = []
+    for side in range(2):
+        at = side_of(d, side)
+        locals_out.append(pltpu.make_async_copy(stage_r.at[side], out_r.at[:, columns(at)], local.at[4 + 2 * side]))
+        locals_out.append(pltpu.make_async_copy(stage_s.at[side], out_s.at[lines(at), :], local.at[5 + 2 * side]))
+    for copy in locals_out:
+        copy.start()
 
     total = gate_part[0]
-    for mask in range(1, n_dp):
+    for mask in range(1, n_low):
         remote(
             gate_recv.at[mask], gate_recv.at[mask], g1_send.at[mask], g1_recv.at[mask], dp_peer(mask)
         ).wait_recv()
@@ -304,27 +362,38 @@
         final = final + gate_last[mask]
     gate_out[...] = final
 
-    for mask in range(1, n_dp):
-        origin = flip(d, mask, dp_bits)
-        from_r = out_r.at[:, pl.ds(pl.multiple_of(origin * hid_r, hid_r), hid_r)]
-        from_s = out_s.at[pl.ds(pl.multiple_of(origin * hid_s, hid_s), hid_s), :]
-        remote(stage_r.at[mask], from_r, outr_send.at[mask], outr_recv.at[mask], dp_peer(mask)).wait()
-        remote(stage_s.at[mask], from_s, outs_send.at[mask], outs_recv.at[mask], dp_peer(mask)).wait()
-        remote(in_r.at[mask], in_r.at[mask], inr_send.at[mask], inr_recv.at[mask], dp_peer(mask)).wait_send()
-        remote(in_s.at[mask], in_s.at[mask], ins_send.at[mask], ins_recv.at[mask], dp_peer(mask)).wait_send()
-        remote(metas.at[d], metas.at[d], m2_send.at[mask], m2_recv.at[mask], dp_peer(mask)).wait_send()
+    for copy in sums:
+        copy.wait()
+    grad_r[...] += got_r[...].astype(jnp.float32)
+    grad_s[...] += got_s[...].astype(jnp.float32)
+
+    for mask in range(1, n_low):
+        for side in range(2):
+            slot = 2 * mask + side
+            origin = side_of(flip(d, mask, dp_bits), side)
+            remote(
+                stage_r.at[slot], out_r.at[:, columns(origin)], outr_send.at[slot], outr_recv.at[slot], dp_peer(mask)
+            ).wait()
+            remote(
+                stage_s.at[slot], out_s.at[lines(origin), :], outs_send.at[slot], outs_recv.at[slot], dp_peer(mask)
+            ).wait()
+            remote(in_r.at[slot], in_r.at[slot], inr_send.at[slot], inr_recv.at[slot], dp_peer(mask)).wait_send()
+            remote(in_s.at[slot], in_s.at[slot], ins_send.at[slot], ins_recv.at[slot], dp_peer(mask)).wait_send()
+        remote(metas.at[low], metas.at[low], m2_send.at[mask], m2_recv.at[mask], dp_peer(mask)).wait_send()
         remote(
             gate_part.at[mask], gate_recv.at[mask], g1_send.at[mask], g1_recv.at[mask], dp_peer(mask)
         ).wait_send()
     for mask in range(1, n_exp):
-        remote(metas.at[d, e], metas.at[d, e], m1_send.at[mask], m1_recv.at[mask], exp_peer(mask)).wait_send()
+        remote(metas.at[low, e], metas.at[low, e], m1_send.at[mask], m1_recv.at[mask], exp_peer(mask)).wait_send()
         remote(
             gate_sum.at[flip(e, mask, exp_bits)], gate_last.at[mask], g2_send.at[mask], g2_recv.at[mask], exp_peer(mask)
         ).wait_send()
-    for mask in range(1, n_dp * n_exp):
+    for mask in range(1, n_low * n_exp):
         arrived(mask).wait_send()
-    last_r.wait()
-    last_s.wait()
+    for copy in weights:
+        copy.wait_send()
+    for copy in locals_out:
+        copy.wait()
 
 
 def token_body(grad_out, expert_ids, gates, routed_pre, routed_down, shared_pre, shared_down):
@@ -345,7 +414,8 @@
     )
     any_spec, vmem = pl.BlockSpec(memory_space=pl.ANY), pl.BlockSpec(memory_space=pltpu.VMEM)
     bf, f32, dma = jnp.bfloat16, jnp.float32, pltpu.SemaphoreType.DMA
-    every = n_dp * n_exp
+    n_low = n_dp // 2
+    every = n_low * n_exp
     flops = 4 * n_dp * width * (slots * hid_r + group * hid_s)
     out_r, out_s, grad_r, grad_s, gate = pl.pallas_call(
         functools.partial(token_kernel, dp_bits, exp_bits, cap),
@@ -360,25 +430,34 @@
         out_specs=[any_spec, any_spec, vmem, vmem, vmem],
         scratch_shapes=[
             pltpu.VMEM((every * tok, width), bf),
-            pltpu.VMEM((n_dp, n_exp, 8, tok), f32),
+            pltpu.VMEM((n_low, n_exp, 8, tok), f32),
             pltpu.VMEM((n_dp, slots, hid_r), bf),
             pltpu.VMEM((n_dp, hid_s, group), bf),
             pltpu.VMEM((n_dp, slots, hid_r), bf),
             pltpu.VMEM((n_dp, hid_s, group), bf),
+            pltpu.VMEM((n_low, slots, width), bf),
             pltpu.VMEM((slots, width), bf),
-            pltpu.VMEM((slots, width), bf),
-            pltpu.VMEM((n_dp, n_exp, 8, tok), f32),
-            pltpu.VMEM((n_dp, n_exp, 8, tok), f32),
+            pltpu.VMEM((2, hid_r, width), bf),
+            pltpu.VMEM((2, hid_s, width), bf),
+            pltpu.VMEM((hid_r, width), f32),
+            pltpu.VMEM((hid_s, width), f32),
+            pltpu.VMEM((hid_r, width), bf),
+            pltpu.VMEM((hid_s, width), bf),
+            pltpu.VMEM((hid_r, width), bf),
+            pltpu.VMEM((hid_s, width), bf),
+            pltpu.VMEM((n_low, n_exp, 8, tok), f32),
+            pltpu.VMEM((n_low, n_exp, 8, tok), f32),
             pltpu.VMEM((n_exp, 8, tok), f32),
             pltpu.VMEM((n_exp, 8, tok), f32),
             dma((every,)), dma((every,)),
             dma((n_exp,)), dma((n_exp,)),
-            dma((n_dp,)), dma((n_dp,)),
+            dma((n_low,)), dma((n_low,)),
             dma((n_dp,)), dma((n_dp,)), dma((n_dp,)), dma((n_dp,)),
             dma((n_dp,)), dma((n_dp,)), dma((n_dp,)), dma((n_dp,)),
-            dma((n_dp,)), dma((n_dp,)),
+            dma((n_low,)), dma((n_low,)),
             dma((n_exp,)), dma((n_exp,)),
-            dma((4,)),
+            dma((4,)), dma((4,)),
+            dma((8,)),
         ],
         compiler_params=pltpu.CompilerParams(
             collective_id=0, has_side_effects=True, vmem_limit_bytes=56 << 20
@@ -397,7 +476,7 @@
 def by_tokens(mesh, shapes):
     n_dp, n_exp = mesh.shape["dp"], mesh.shape["expert"]
     tokens, (hidden, shared) = shapes[0][0], (shapes[4][1], shapes[6][0])
-    powers = n_dp & (n_dp - 1) == 0 and n_exp & (n_exp - 1) == 0
+    powers = n_dp > 1 and n_dp & (n_dp - 1) == 0 and n_exp & (n_exp - 1) == 0
     aligned = hidden % (128 * n_dp) == 0 and shared % (16 * n_dp * n_exp) == 0
     return powers and aligned and tokens <= hidden + shared // n_exp
 

time: 246 us -> 206 us (0.84)
  Pallas kernels: 229 us -> 190 us
    pallas_call x1, Pallas kernels: 229 us -> 190 us  [token_body(): pl.pallas_call(functools.partial(token_kernel, dp_bits, exp_bits, cap), o...]
where the time goes in v3:
time: 206 us
  Pallas kernels  190 us (92%)
  local copies, waits for them, and re-layouts  13.4 us (7%)
  other arithmetic  2.23 us (1%)
    pallas_call x1, Pallas kernels, token_body(): pl.pallas_call(functools.partial(token_kernel, dp_bits, exp_bits, cap), o...  190 us
    unnamed x12, local copies, waits for them, and re-layouts  11.7 us

profile of v3, /device:TPU:0, one launch (start us, length us, event | category | flops | bytes accessed | tf_op | source)
XLA Modules:
  0.0 206.0 jit_solution(3064196657316305488)
XLA Ops:
  0.6 0.1 pad.3.clone
  0.7 0.7 convert_bitcast_fusion
  1.4 0.8 copy.18
  2.2 0.1 eq.15
  2.3 0.2 convert_reduce_fusion
  2.5 0.1 reshape.18
  2.7 0.1 copy.19
  2.7 1.4 maximum_maximum_fusion.meta
  4.1 2.6 %copy.20 = bf16[512,1536]{0,1:T(8,128)(2,1)} copy(bf16[512,1536]{1,0:T(8,128)(2,1)} %param.12) | data formatting | bytes 3145728 | tf_op args[5]
  6.7 189.7 %shard_map.110 = (bf16[384,3072]{1,0:T(8,128)(2,1)}, bf16[1536,512]{1,0:T(8,128)(2,1)}, f32[384,1536]{1,0:T(8,128)}, f32[192,1536]{1,0:T(8,128)}, f32[8,128]{1,0:T(8,128)}) custom-call(bf16[128,1536]{1,0:T(8,128)(2,1)} %grad.1, f32[8,128]{1,0:T(8,128)} %maximum_maximum_fusion.meta, bf16[384,3072]{1,0:T(8,128)(2,1)} %bitcast.18, bf16[1536,512]{1,0:T(8,128)(2,1)} %bitcast.15, ...), custom_call_target="tpu_custom_call" | custom-call | flops 12079595520 | bytes 16777216 | tf_op jit(solution)/shard_map/pallas_call | solution.py:420
  196.4 1.2 slice_bitcast_fusion
  197.6 0.0 copy-start.1
  197.6 2.7 %copy.21 = bf16[512,1536]{1,0:T(8,128)(2,1)} copy(bf16[512,1536]{0,1:T(8,128)(2,1)} %bitcast.14) | data formatting | bytes 3145728
  200.4 0.0 copy-done.1
  200.4 0.0 copy-start
  200.4 1.4 copy.25
  201.8 1.1 copy-done
  202.9 0.0 copy-start.2
  202.9 1.4 copy.26
  204.3 0.7 copy-done.2
  205.0 1.0 copy.27
  (1 shorter events, 0.0 us)
Async XLA Ops:
  197.6 2.7 %copy-start.1 = (bf16[384,3072]{1,0:T(8,128)(2,1)S(1)}, bf16[384,3072]{1,0:T(8,128)(2,1)}, u32[]{:S(2)}) copy-start(bf16[384,3072]{1,0:T(8,128)(2,1)} %get-tuple-element.10) | copy-start | bytes 7077892
  200.4 2.5 %copy-start = (f32[384,1536]{1,0:T(8,128)S(1)}, f32[384,1536]{1,0:T(8,128)}, u32[]{:S(2)}) copy-start(f32[384,1536]{1,0:T(8,128)} %get-tuple-element.11) | copy-start | bytes 7077892
  202.9 2.1 %copy-start.2 = (f32[192,1536]{1,0:T(8,128)S(1)}, f32[192,1536]{1,0:T(8,128)}, u32[]{:S(2)}) copy-start(f32[192,1536]{1,0:T(8,128)} %get-tuple-element.38) | copy-start | bytes 3538948
